TPU v7x, 32 devices: a whole 2x2x4 slice. The times are simulated.
32 devices in a mesh: ka: 8 (over z, core), kp: 4 (over y, x).
Axes of the slice: x: 2, y: 2, z: 4, core: 2. Of those that a mesh axis runs over, the one named last changes fastest.
Arguments:
- cond_pairs: bfloat16 [128, 512, 16], P(('ka', 'kp')), may hold values from -0.5 to 0.5
- val_pairs: bfloat16 [128, 512, 16], P('kp'), may hold values from -0.5 to 0.5
- w_store: bfloat16 [64, 512, 512], P('ka')
- q_table: int32 [128, 64], P(('ka', 'kp')), may hold values from 0 to 255, as said below
- q_to_irr: int32 [256], replicated, may hold values from 0 to 63, as said below
- g_perm: int32 [256, 512], replicated, may hold values from 0 to 511, each once within a row
- home_slot: int32 [64], replicated, may hold values from 0 to 63, as said below
Outputs:
- kernel_window: float32 [2048, 1024], P(('ka', 'kp'))
Inputs may be any that keep to these rules, and one draw needn't show every extreme that they name: `q_to_irr`: each irreducible index is named by exactly 4 momentum transfers. `home_slot`: A permutation of the storage positions. `g_perm`: each row is a permutation of the plane waves. `q_table`: for the 4 rows of one device and either half of the columns, the transfers name at most one irreducible block whose storage position lies in each run of 8 positions, and at most 24 slots name the same irreducible block; the second bound is reached for every device and half.
All inputs are finite; a program needn't handle non-finite values.
Results may differ from a plain program's by a relative error of at most 0.003.
Values may be sent and summed in bfloat16 or wider, within the bound.
A program may use at most 128 MiB of HBM per device.

v0:
```python
import jax
import jax.numpy as jnp
from jax import lax
from jax.sharding import PartitionSpec as P

NSYM = 4


def passed_along(shard, axis, by):
    peers = lax.axis_size(axis)
    return lax.ppermute(shard, axis, [(i, (i + by) % peers) for i in range(peers)])


def need_list(q_part, q_to_irr, home_slot, owners, per_owner):
    stored = home_slot[q_to_irr[q_part]]
    owner_of = stored // per_owner
    slot_index = stored % per_owner
    member = (owner_of[:, None] == jnp.arange(owners, dtype=jnp.int32)[None, :]).astype(jnp.int32)
    requested_rows = jnp.max(member * slot_index[:, None], axis=0)
    return (owner_of, member, requested_rows)


def pair_slots(owner_of, member, owners, capacity):
    pair_count = owner_of.shape[0]
    before = jnp.cumsum(member, axis=0) - member
    position = jnp.sum(before * member, axis=1)
    flat_slot = owner_of * capacity + position
    pair_ids = jnp.arange(pair_count, dtype=jnp.int32)
    slot_ids = jnp.arange(owners * capacity, dtype=jnp.int32)
    placed = (flat_slot[:, None] == slot_ids[None, :]).astype(jnp.int32)
    pair_table = jnp.sum(placed * pair_ids[:, None], axis=0)
    return (flat_slot, pair_table.reshape(owners, capacity))


def pair_products(one_block, chosen, panel_t, cond_t, q_part, q_to_irr, g_perm):
    width = panel_t.shape[1]
    row_count = cond_t.shape[1]
    pair_q = q_part[chosen]
    block_irr = q_to_irr[pair_q[0]]
    candidates = jnp.nonzero(q_to_irr == block_irr, size=NSYM, fill_value=0)[0].astype(jnp.int32)
    col_of = chosen % width
    row_of = chosen // width
    col_ids = jnp.arange(width, dtype=jnp.int32)
    row_ids = jnp.arange(row_count, dtype=jnp.int32)
    val_sum = None
    cond_sum = None
    for image in range(NSYM):
        target = candidates[image]
        shuffle = g_perm[target]
        matched = pair_q == target
        valence_permutation = panel_t[shuffle]
        conduction_permutation = cond_t[shuffle]
        select_valence = ((col_of[None, :] == col_ids[:, None]) & matched[None, :]).astype(
            jnp.bfloat16
        )
        select_conduction = ((row_of[None, :] == row_ids[:, None]) & matched[None, :]).astype(
            jnp.bfloat16
        )
        valence_factor = jnp.einsum(
            "kuf,uq->kqf", valence_permutation, select_valence, preferred_element_type=jnp.float32
        )
        cond_term = jnp.einsum(
            "kuf,uq->kqf",
            conduction_permutation,
            select_conduction,
            preferred_element_type=jnp.float32,
        )
        val_sum = valence_factor if val_sum is None else val_sum + valence_factor
        cond_sum = cond_term if cond_sum is None else cond_sum + cond_term
    val_rows = val_sum.astype(jnp.bfloat16)
    cond_rows = cond_sum.astype(jnp.bfloat16)
    carried = jnp.einsum(
        "gh,hnp->gnp", one_block, val_rows, preferred_element_type=jnp.float32
    ).astype(jnp.bfloat16)
    return -jnp.einsum("gni,gnj->nij", cond_rows, carried, preferred_element_type=jnp.float32)


def assemble(results, flat_slot, row_count, width, band_pairs):
    per_pair = results[flat_slot]
    per_pair = per_pair.reshape(row_count, width, band_pairs, band_pairs).transpose(0, 2, 1, 3)
    return per_pair.reshape(row_count * band_pairs, width * band_pairs)


def stop_kernel(blocks, panel_t, cond_t, q_part, q_to_irr, g_perm, owner_of, member):
    owners = blocks.shape[0]
    row_count = cond_t.shape[1]
    width = panel_t.shape[1]
    band_pairs = cond_t.shape[2]
    capacity = 3 * row_count * row_count // 2
    flat_slot, pair_table = pair_slots(owner_of, member, owners, capacity)

    def one_owner(inputs):
        one_block, chosen = inputs
        return pair_products(one_block, chosen, panel_t, cond_t, q_part, q_to_irr, g_perm)

    results = lax.map(one_owner, (blocks, pair_table))
    results = results.reshape(owners * capacity, band_pairs, band_pairs)
    return assemble(results, flat_slot, row_count, width, band_pairs)


def per_device(cond_pairs, val_pairs, w_store, q_table, q_to_irr, g_perm, home_slot):
    owners = lax.axis_size("ka")
    per_owner = w_store.shape[0]
    width = val_pairs.shape[0]
    shifted = passed_along(val_pairs, "kp", 1)
    panels_t = (val_pairs.transpose(1, 0, 2), shifted.transpose(1, 0, 2))
    cond_t = cond_pairs.transpose(1, 0, 2)
    q_parts = (q_table[:, :width].reshape(-1), q_table[:, width:].reshape(-1))
    needs = [need_list(q_parts[stop], q_to_irr, home_slot, owners, per_owner) for stop in range(2)]
    results = []
    for stop in range(2):
        owner_of, member, requested_rows = needs[stop]
        asked_for = lax.all_to_all(requested_rows, "ka", split_axis=0, concat_axis=0, tiled=True)
        departing_rows = w_store[asked_for]
        blocks = lax.all_to_all(departing_rows, "ka", split_axis=0, concat_axis=0, tiled=True)
        results.append(
            stop_kernel(
                blocks, panels_t[stop], cond_t, q_parts[stop], q_to_irr, g_perm, owner_of, member
            )
        )
    return jnp.concatenate(results, axis=1)


def solution(mesh):
    placed = (
        P(("ka", "kp"), None, None),
        P("kp", None, None),
        P("ka", None, None),
        P(("ka", "kp"), None),
        P(),
        P(),
        P(),
    )
    return jax.shard_map(
        per_device, mesh=mesh, in_specs=placed, out_specs=P(("ka", "kp"), None), check_vma=False
    )
```

profile of v0, /device:TPU:9, one launch (start us, length us, event | category | flops | bytes accessed | tf_op | source)
XLA Modules:
  0.0 1262.4 jit_solution(11940495441524913363)
XLA Ops:
  5.0 5.6 all-to-all-start.2
  14.7 5.1 all-to-all-start
  20.1 4.9 gather_fusion.24
  25.0 5.2 all-to-all-start.3
  35.5 5.0 gather_fusion.20
  40.5 4.0 collective-permute-done
  44.5 4.6 copy.124
  49.1 71.6 %all-to-all-done.3 = bf16[8,512,512]{2,1,0:T(8,128)(2,1)} async-done(((bf16[8,512,512]{2,1,0:T(8,128)(2,1)}), bf16[8,512,512]{2,1,0:T(8,128)(2,1)}, u32[]{:S(2)}, u32[]{:S(2)}) %all-to-all-start.3) | async-done | bytes 4194336 | tf_op jit(solution)/shard_map/all_to_all | solution.py:115
  120.7 8.1 all-to-all-start.1
  130.1 578.8 %while.27 = (s32[]{:T(128)}, f32[8,24,16,16]{3,2,1,0:T(8,128)}, s32[8,24]{1,0:T(8,128)S(1)}, s32[128]{0:T(128)S(1)}, s32[256]{0:T(256)S(1)}, /*index=5*/s32[256,...) while((s32[]{:T(128)}, f32[8,24,16,16]{3,2,1,0:T(8,128)}, ...), condition=%wide.region_21.22_spmd, body=%wide.region_15.21_spmd.sunk | while | flops 266070816 | bytes 21767976 | solution.py:96
  146.3 4.0 gather_fusion.14
  155.2 4.0 gather_fusion.15
  162.5 4.0 gather_fusion.16
  169.8 4.0 gather_fusion.17
  218.6 4.0 gather_fusion.14
  227.5 4.0 gather_fusion.15
  234.8 4.0 gather_fusion.16
  242.1 4.0 gather_fusion.17
  291.0 4.0 gather_fusion.14
  299.9 4.0 gather_fusion.15
  307.2 4.0 gather_fusion.16
  314.5 4.0 gather_fusion.17
  363.3 4.0 gather_fusion.14
  372.2 4.0 gather_fusion.15
  379.5 4.0 gather_fusion.16
  386.8 4.0 gather_fusion.17
  435.7 4.0 gather_fusion.14
  444.6 4.0 gather_fusion.15
  451.9 4.0 gather_fusion.16
  459.2 4.0 gather_fusion.17
  508.0 4.0 gather_fusion.14
  517.0 4.0 gather_fusion.15
  524.2 4.0 gather_fusion.16
  531.5 4.0 gather_fusion.17
  580.4 4.0 gather_fusion.14
  589.3 4.0 gather_fusion.15
  596.6 4.0 gather_fusion.16
  603.9 4.0 gather_fusion.17
  652.7 4.0 gather_fusion.14
  661.7 4.0 gather_fusion.15
  668.9 4.0 gather_fusion.16
  676.2 4.0 gather_fusion.17
  719.0 538.9 %while.26 = (s32[]{:T(128)}, f32[8,24,16,16]{3,2,1,0:T(8,128)}, s32[8,24]{1,0:T(8,128)S(1)}, s32[128]{0:T(128)S(1)}, s32[256]{0:T(256)S(1)}, /*index=5*/s32[256,...) while((s32[]{:T(128)}, f32[8,24,16,16]{3,2,1,0:T(8,128)}, ...), condition=%wide.region_10.11_spmd, body=%wide.region_4.10_spmd.sunk | while | flops 266070816 | bytes 21767976 | solution.py:96
  886.2 3.4 fusion.288
  953.5 3.4 fusion.288
  1088.3 3.4 fusion.288
  1155.7 3.4 fusion.288
  1223.0 3.4 fusion.288
  (803 shorter events, 880.3 us)
Async XLA Ops:
  0.0 2.6 copy-start
  5.0 9.8 all-to-all-start.2
  14.7 10.3 all-to-all-start
  25.0 5.2 copy-start.3
  25.0 95.7 %all-to-all-start.3 = ((bf16[8,512,512]{2,1,0:T(8,128)(2,1)}), bf16[8,512,512]{2,1,0:T(8,128)(2,1)}, u32[]{:S(2)}, u32[]{:S(2)}) async-start(bf16[8,512,512]{2,1,0:T(8,128)(2,1)} %gather_fusion.24), calls=%async_computation.3 | async-start | bytes 8388608 | tf_op jit(solution)/shard_map/all_to_all | solution.py:115
  30.3 3.8 copy-start.5
  30.3 14.2 %collective-permute-start = (bf16[32,512,16]{1,2,0:T(8,128)(2,1)S(1)}, bf16[32,512,16]{1,2,0:T(8,128)(2,1)}, u32[]{:S(2)}, u32[]{:S(2)}) collective-permute-start(bf16[32,512,16]{1,2,0:T(8,128)(2,1)S(1)} %copy-done.3), channel_id=1, source_target_pairs={{0,1},{1,2},{2,3},{3,0},{4,5},{5,6},{6,7},{7,4},{8,9},{9,10},{10,1... | collective-permute-start | bytes 1572872 | tf_op jit(solution)/shard_map/ppermute | solution.py:11
  49.1 81.0 %copy-start.2 = (s32[256]{0:T(256)S(1)}, s32[256]{0:T(256)}, u32[]{:S(2)}) copy-start(s32[256]{0:T(256)} %param.15) | copy-start | bytes 3076
  120.7 597.0 %all-to-all-start.1 = ((bf16[8,512,512]{2,1,0:T(8,128)(2,1)}), bf16[8,512,512]{2,1,0:T(8,128)(2,1)}, u32[]{:S(2)}, u32[]{:S(2)}) async-start(bf16[8,512,512]{2,1,0:T(8,128)(2,1)} %gather_fusion.20), calls=%async_computation.1 | async-start | bytes 8388608 | tf_op jit(solution)/shard_map/all_to_all | solution.py:115
  1260.1 2.3 copy-start.1
  1260.1 1.6 copy-start.4
where the time goes:
time: 1280 us; the launch traced here: 1260 us
  local copies, waits for them, and re-layouts  543 us (42%)
  matrix products  350 us (27%)
  other arithmetic  144 us (11%)
  loops' own time  124 us (10%)
  waiting for transfers between devices  75.6 us (6%)
  starting transfers between devices  25.3 us (2%)
    gather x128, local copies, waits for them, and re-layouts, pair_products(): conduction_permutation = cond_t[shuffle]  251 us
    gather x64, local copies, waits for them, and re-layouts, pair_products(): valence_permutation = panel_t[shuffle]  215 us
    dot_general x64, matrix products, pair_products(): jnp.einsum('kuf,uq->kqf', valence_permutation, select_valence, preferred_...  192 us
    another operation x2, loops' own time, stop_kernel(): results = lax.map(one_owner, (blocks, pair_table))  124 us
    dot_general x64, matrix products, pair_products(): jnp.einsum('kuf,uq->kqf', conduction_permutation, select_conduction, pref...  119 us
    all_to_all x2, waiting for transfers between devices, per_device(): lax.all_to_all(departing_rows, 'ka', split_axis=0, concat_axis=0, tiled=T...  71.6 us
    eq x16, other arithmetic, pair_products(): matched = pair_q == target  39.9 us
    scatter-add x16, other arithmetic, pair_products(): jnp.nonzero(q_to_irr == block_irr, size=NSYM, fill_value=0)[0]  37.1 us
  transfers between devices with their start and end apart: 5, of which 2 were waited for; matrix products, arithmetic and copies ran while one was open for 44% of the time, Pallas kernels for 0%

commit v1 on v0

v1 whole, which is shorter than its diff:
```python
import functools

import jax
import jax.numpy as jnp
from jax import lax
from jax.experimental import pallas as pl
from jax.experimental.pallas import tpu as pltpu
from jax.sharding import PartitionSpec as P

NSYM = 4
CHUNK = 8


def pair_lists(q_all, q_to_irr, home_slot, per_owner, capacity):
    me = lax.axis_index("ka")
    i32 = jnp.int32
    irr_ids = jnp.arange(home_slot.shape[0], dtype=i32)
    stored = jnp.sum(
        jnp.where(q_to_irr[:, None] == irr_ids[None, :], home_slot[None, :], 0), axis=1
    )
    member = (stored // per_owner) == me
    q_count = q_to_irr.shape[0]
    q_ids = jnp.arange(q_count, dtype=i32)
    local_q = per_owner * NSYM
    rank = jnp.sum((member[None, :] & (q_ids[None, :] < q_ids[:, None])).astype(i32), axis=1)
    t_ids = jnp.arange(local_q, dtype=i32)
    at_t = member[None, :] & (rank[None, :] == t_ids[:, None])
    q_of = jnp.sum(jnp.where(at_t, q_ids[None, :], 0), axis=1)
    block_of = jnp.sum(jnp.where(at_t, stored[None, :] % per_owner, 0), axis=1)

    pairs = q_all.reshape(-1)
    pair_count = pairs.shape[0]
    run = 128
    same = (pairs.reshape(1, -1, run) == q_of[:, None, None])
    before = (jnp.arange(run)[:, None] < jnp.arange(run)[None, :]).astype(jnp.bfloat16)
    within = lax.dot_general(
        same.astype(jnp.bfloat16).reshape(-1, run), before, (((1,), (0,)), ((), ())),
        preferred_element_type=jnp.float32,
    ).astype(i32).reshape(same.shape)
    per_run = jnp.sum(same.astype(i32), axis=2)
    runs = per_run.shape[1]
    run_ids = jnp.arange(runs, dtype=i32)
    run_start = jnp.sum(
        jnp.where(run_ids[None, :, None] > run_ids[None, None, :], per_run[:, None, :], 0), axis=2
    )
    count = jnp.sum(per_run, axis=1)
    chunks = (count + CHUNK - 1) // CHUNK
    first = jnp.sum(jnp.where(t_ids[:, None] > t_ids[None, :], chunks[None, :], 0), axis=1)
    place = (first * CHUNK)[:, None, None] + run_start[:, :, None] + within
    position = jnp.sum(jnp.where(same, place + 1, 0), axis=0).reshape(-1) - 1
    slots = capacity + local_q * CHUNK
    slot_ids = jnp.arange(slots, dtype=i32)
    pair_ids = jnp.arange(pair_count, dtype=i32)
    table = jnp.sum(
        jnp.where(position[None, :] == slot_ids[:, None], pair_ids[None, :] + 1, 0), axis=1
    ) - 1
    meta = jnp.stack([q_of, block_of, first, chunks])
    return table, meta


def owner_kernel(table, meta, val_ref, cond_ref, w_ref, perm_ref, out_ref, rows, shuffle):
    half = CHUNK * 16
    g = w_ref.shape[1]
    columns = val_ref.shape[0]
    local_q = meta.shape[1]
    out_ref[...] = jnp.zeros_like(out_ref)
    lane_group = lax.broadcasted_iota(jnp.int32, (16, 128), 1) // 16

    def one_transfer(t, carry):
        chunks = meta[3, t]

        @pl.when(chunks > 0)
        def _():
            order = perm_ref[pl.ds(meta[0, t], 1), :]
            g_ids = lax.broadcasted_iota(jnp.int32, (g, g), 0)
            shuffle[...] = jnp.where(g_ids == order, 1.0, 0.0).astype(jnp.bfloat16)
            block = meta[1, t]

            def one_chunk(step, inner):
                base = (meta[2, t] + step) * CHUNK
                for p in range(CHUNK):
                    pair = jnp.maximum(table[base + p], 0)
                    rows[p * 16:(p + 1) * 16, :] = val_ref[pair % columns]
                    rows[half + p * 16:half + (p + 1) * 16, :] = cond_ref[pair // columns]
                moved = jnp.dot(
                    rows[...], shuffle[...], preferred_element_type=jnp.float32
                ).astype(jnp.bfloat16)
                carried = lax.dot_general(
                    moved[:half], w_ref[block], (((1,), (1,)), ((), ())),
                    preferred_element_type=jnp.float32,
                ).astype(jnp.bfloat16)
                products = -lax.dot_general(
                    moved[half:], carried, (((1,), (1,)), ((), ())),
                    preferred_element_type=jnp.float32,
                )
                for p in range(CHUNK):
                    pair = table[base + p]

                    @pl.when(pair >= 0)
                    def _(p=p, pair=pair):
                        row, col = pair // columns, pair % columns
                        group = col % 8
                        turned = pltpu.roll(
                            products[p * 16:(p + 1) * 16, :], ((group - p + 8) % 8) * 16, 1
                        ).astype(jnp.bfloat16)
                        at = pl.ds(pl.multiple_of((col // 8) * 128, 128), 128)
                        out_ref[row, :, at] = jnp.where(
                            lane_group == group, turned, out_ref[row, :, at]
                        )
                return inner

            lax.fori_loop(0, chunks, one_chunk, 0)
        return carry

    lax.fori_loop(0, local_q, one_transfer, 0)


def owner_products(table, meta, val_t, cond_t, w_store, g_perm):
    rows, band_pairs, g = cond_t.shape
    columns = val_t.shape[0]
    vmem = pl.BlockSpec(memory_space=pltpu.VMEM)
    smem = pl.BlockSpec(memory_space=pltpu.SMEM)
    return pl.pallas_call(
        owner_kernel,
        out_shape=jax.ShapeDtypeStruct((rows, band_pairs, columns * band_pairs), jnp.bfloat16),
        in_specs=[smem, smem, vmem, vmem, vmem, vmem],
        out_specs=vmem,
        scratch_shapes=[
            pltpu.VMEM((2 * CHUNK * band_pairs, g), jnp.bfloat16),
            pltpu.VMEM((g, g), jnp.bfloat16),
        ],
        compiler_params=pltpu.CompilerParams(vmem_limit_bytes=48 * 1024 * 1024),
        cost_estimate=pl.CostEstimate(
            flops=10_000_000_000, bytes_accessed=8_000_000, transcendentals=0
        ),
    )(table, meta, val_t, cond_t, w_store, g_perm)


def per_device(cond_pairs, val_pairs, w_store, q_table, q_to_irr, g_perm, home_slot):
    owners = lax.axis_size("ka")
    peers = lax.axis_size("kp")
    per_owner = w_store.shape[0]
    row_count = cond_pairs.shape[0]
    band_pairs = cond_pairs.shape[2]
    q_all = lax.all_gather(q_table, "ka", axis=0, tiled=True)
    cond_t = lax.all_gather(cond_pairs.transpose(0, 2, 1), "ka", axis=0, tiled=True)
    own_t = val_pairs.transpose(0, 2, 1)
    next_t = lax.ppermute(own_t, "kp", [(i, (i + 1) % peers) for i in range(peers)])
    val_t = jnp.concatenate([own_t, next_t], axis=0)
    capacity = owners * 2 * (3 * row_count * row_count // 2)
    table, meta = pair_lists(q_all, q_to_irr, home_slot, per_owner, capacity)
    parts = owner_products(table, meta, val_t, cond_t, w_store, g_perm)
    columns = val_t.shape[0] * band_pairs
    parts = parts.reshape(owners, row_count * band_pairs, columns)
    back = lax.all_to_all(parts, "ka", split_axis=0, concat_axis=0, tiled=True)
    return jnp.sum(back.astype(jnp.float32), axis=0)


def solution(mesh):
    placed = (
        P(("ka", "kp"), None, None),
        P("kp", None, None),
        P("ka", None, None),
        P(("ka", "kp"), None),
        P(),
        P(),
        P(),
    )
    return jax.shard_map(
        per_device, mesh=mesh, in_specs=placed, out_specs=P(("ka", "kp"), None), check_vma=False
    )
```

time: 1280 us -> 127 us (0.10)
  the two profiles are of different devices: /device:TPU:9 before, /device:TPU:0 now
where the time goes in v1:
time: 127 us; the launch traced here: 124 us
  blocking collectives  62.1 us (49%)
  Pallas kernels  52.2 us (41%)
  other arithmetic  5.51 us (4%)
  starting transfers between devices  2.94 us (2%)
  local copies, waits for them, and re-layouts  1.41 us (1%)
    pallas_call x1, Pallas kernels, owner_products(): pl.pallas_call(owner_kernel, out_shape=jax.ShapeDtypeStruct((rows, band_p...  52.2 us
    all_to_all x1, blocking collectives, per_device(): back = lax.all_to_all(parts, 'ka', split_axis=0, concat_axis=0, tiled=True)  34.1 us
    all_gather x1, blocking collectives, per_device(): lax.all_gather(cond_pairs.transpose(0, 2, 1), 'ka', axis=0, tiled=True)  14.9 us
    all_gather x1, blocking collectives, per_device(): q_all = lax.all_gather(q_table, 'ka', axis=0, tiled=True)  13.1 us
    ppermute x1, starting transfers between devices, per_device(): lax.ppermute(own_t, 'kp', [(i, (i + 1) % peers) for i in range(peers)])  2.94 us
  transfers between devices with their start and end apart: 1, of which 0 were waited for; matrix products, arithmetic and copies ran while one was open for 3% of the time, Pallas kernels for 0%

profile of v1, /device:TPU:0, one launch (start us, length us, event | category | flops | bytes accessed | tf_op | source)
XLA Modules:
  0.0 124.4 jit_solution(1150795554145828017)
XLA Ops:
  0.0 2.9 %collective-permute-start = (bf16[32,16,512]{2,1,0:T(8,128)(2,1)}, bf16[32,16,512]{2,1,0:T(8,128)(2,1)S(1)}, u32[]{:S(2)}, u32[]{:S(2)}) collective-permute-start(bf16[32,16,512]{2,1,0:T(8,128)(2,1)} %bitcast.23), channel_id=1, source_target_pairs={{0,1},{1,2},{2,3},{3,0},{4,5},{5,6},{6,7},{7,4},{8,9},{9,10},{10,1... | collective-permute-start | bytes 1572872 | tf_op jit(solution)/shard_map/ppermute | solution.py:148
  3.0 0.8 select_reduce_fusion.2
  3.8 0.1 convert_reduce_fusion.3
  3.9 13.1 %all-gather = s32[8,4,64]{2,1,0:T(4,128)S(1)} all-gather(s32[1,4,64]{2,1,0:T(4,128)} %bitcast.27), channel_id=1, replica_groups=mesh['ka'=8,'kp'=4] {'ka'}, dimensions={0}, use_global_device_ids=true | all-gather | bytes 9216 | tf_op jit(solution)/shard_map/all_gather | solution.py:145
  17.0 0.1 eq.77
  17.0 0.1 select_reduce_fusion.3
  17.2 1.3 %convert_reduce_fusion.2 = (s32[32]{0:T(128)S(1)}, s32[32,16]{1,0:T(8,128)S(1)}) fusion(s32[16,128]{1,0:T(8,128)S(1)} %eq.77, s32[32]{0:T(128)S(1)} %get-tuple-element.8), kind=kLoop, calls=%fused_computation.6 | loop fusion | flops 261600 | bytes 10496 | tf_op jit(solution)/shard_map/reduce_sum | solution.py:46
  18.5 0.1 eq.90
  18.5 0.1 eq.91
  18.6 0.1 copy.9
  18.7 0.1 select_reduce_fusion.5
  18.8 0.1 select_reduce_fusion.1
  18.9 0.1 copy.10
  19.0 0.1 bitcast_compare_fusion
  19.2 0.2 convolution_convert_fusion
  19.4 0.2 fusion
  19.5 0.6 select_reduce_fusion
  20.2 14.9 %all_gather.7.cond_ref = bf16[32,16,512]{2,1,0:T(8,128)(2,1)S(1)} all-gather(bf16[4,16,512]{2,1,0:T(8,128)(2,1)} %bitcast.25), channel_id=1, replica_groups=mesh['ka'=8,'kp'=4] {'ka'}, dimensions={0}, use_global_device_ids=true | all-gather | bytes 589824 | tf_op jit(solution)/shard_map/all_gather | solution.py:146
  35.1 0.0 collective-permute-done
  35.1 1.1 pad_maximum_fusion.val_ref
  36.2 0.0 copy-start
  36.2 1.0 copy-done
  37.3 52.2 %shard_map.73 = bf16[32,16,1024]{2,1,0:T(8,128)(2,1)S(1)} custom-call(s32[640]{0:T(1024)S(1)} %broadcast_add_fusion.1.table, s32[4,32]{1,0:T(4,128)S(1)} %pad_add_fusion.meta, bf16[64,16,512]{2,1,0:T(8,128)(2,1)S(1)} %pad_maximum_fusion.val_ref, bf16[32,16,512]{2,1,0:T(8,128)(2,1)S(1)} %all_gather.7.cond_ref, bf16[8,512,512]{2,1,0:T(8,128)(2,1)} %w_ref.1, ...), custom_call_target="tpu_custom_call" | custom-call | flops 10000000000 | bytes 8000000 | tf_op jit(solution)/shard_map/pallas_call | solution.py:123
  89.5 34.1 %all_to_all.5 = bf16[8,64,1024]{2,1,0:T(8,128)(2,1)S(1)} all-to-all(bf16[8,64,1024]{2,1,0:T(8,128)(2,1)S(1)} %bitcast.21), channel_id=1, replica_groups=mesh['ka'=8,'kp'=4] {'ka'}, dimensions={0} | all-to-all | bytes 2097152 | tf_op jit(solution)/shard_map/all_to_all | solution.py:155
  123.6 0.9 convert_reduce_fusion
  (11 shorter events, 0.1 us)
Async XLA Ops:
  0.0 35.1 %collective-permute-start = (bf16[32,16,512]{2,1,0:T(8,128)(2,1)}, bf16[32,16,512]{2,1,0:T(8,128)(2,1)S(1)}, u32[]{:S(2)}, u32[]{:S(2)}) collective-permute-start(bf16[32,16,512]{2,1,0:T(8,128)(2,1)} %bitcast.23), channel_id=1, source_target_pairs={{0,1},{1,2},{2,3},{3,0},{4,5},{5,6},{6,7},{7,4},{8,9},{9,10},{10,1... | collective-permute-start | bytes 1572872 | tf_op jit(solution)/shard_map/ppermute | solution.py:148
  36.2 1.0 copy-start

commit v2 on v1

v2 whole, which is shorter than its diff:
```python
import functools

import jax
import jax.numpy as jnp
from jax import lax
from jax.experimental import pallas as pl
from jax.experimental.pallas import tpu as pltpu
from jax.sharding import PartitionSpec as P

NSYM = 4
CHUNK = 8
MESH = pl.DeviceIdType.MESH


def pair_lists(q_all, q_to_irr, home_slot, per_owner, capacity):
    me = lax.axis_index("ka")
    i32 = jnp.int32
    irr_ids = jnp.arange(home_slot.shape[0], dtype=i32)
    stored = jnp.sum(
        jnp.where(q_to_irr[:, None] == irr_ids[None, :], home_slot[None, :], 0), axis=1
    )
    member = (stored // per_owner) == me
    q_count = q_to_irr.shape[0]
    q_ids = jnp.arange(q_count, dtype=i32)
    local_q = per_owner * NSYM
    rank = jnp.sum((member[None, :] & (q_ids[None, :] < q_ids[:, None])).astype(i32), axis=1)
    t_ids = jnp.arange(local_q, dtype=i32)
    at_t = member[None, :] & (rank[None, :] == t_ids[:, None])
    q_of = jnp.sum(jnp.where(at_t, q_ids[None, :], 0), axis=1)
    block_of = jnp.sum(jnp.where(at_t, stored[None, :] % per_owner, 0), axis=1)

    pairs = q_all.reshape(-1)
    pair_count = pairs.shape[0]
    run = 128
    same = (pairs.reshape(1, -1, run) == q_of[:, None, None])
    before = (jnp.arange(run)[:, None] < jnp.arange(run)[None, :]).astype(jnp.bfloat16)
    within = lax.dot_general(
        same.astype(jnp.bfloat16).reshape(-1, run), before, (((1,), (0,)), ((), ())),
        preferred_element_type=jnp.float32,
    ).astype(i32).reshape(same.shape)
    per_run = jnp.sum(same.astype(i32), axis=2)
    runs = per_run.shape[1]
    run_ids = jnp.arange(runs, dtype=i32)
    run_start = jnp.sum(
        jnp.where(run_ids[None, :, None] > run_ids[None, None, :], per_run[:, None, :], 0), axis=2
    )
    count = jnp.sum(per_run, axis=1)
    chunks = (count + CHUNK - 1) // CHUNK
    first = jnp.sum(jnp.where(t_ids[:, None] > t_ids[None, :], chunks[None, :], 0), axis=1)
    place = (first * CHUNK)[:, None, None] + run_start[:, :, None] + within
    position = jnp.sum(jnp.where(same, place + 1, 0), axis=0).reshape(-1) - 1
    slots = capacity + local_q * CHUNK
    slot_ids = jnp.arange(slots, dtype=i32)
    pair_ids = jnp.arange(pair_count, dtype=i32)
    filled = jnp.sum(
        jnp.where(position[None, :] == slot_ids[:, None], pair_ids[None, :] + 1, 0), axis=1
    ).reshape(-1, CHUNK)
    table = jnp.where(filled > 0, filled, filled[:, :1]).reshape(-1) - 1
    table = jnp.maximum(table, 0)
    chunk_ids = jnp.arange(slots // CHUNK, dtype=i32)
    of_chunk = (first[:, None] <= chunk_ids[None, :]) & (
        chunk_ids[None, :] < (first + chunks)[:, None]
    )
    chunk_q = jnp.sum(jnp.where(of_chunk, q_of[:, None], 0), axis=0)
    chunk_block = jnp.sum(jnp.where(of_chunk, block_of[:, None], 0), axis=0)
    used = jnp.broadcast_to(jnp.sum(chunks), chunk_q.shape)
    return table, jnp.stack([chunk_q, chunk_block, used])


def owner_kernel(table, meta, val_ref, cond_ref, w_ref, perm_ref, out_ref,
                 rows_a, rows_b, moved_a, moved_b, shuffle_a, shuffle_b):
    half = CHUNK * 16
    g = w_ref.shape[1]
    columns = val_ref.shape[0]
    chunks = meta[2, 0]
    lane_group = lax.broadcasted_iota(jnp.int32, (16, 128), 1) // 16
    out_ref[...] = jnp.zeros_like(out_ref)

    def row_col(pair):
        if columns & (columns - 1) == 0:
            return pair >> (columns.bit_length() - 1), pair & (columns - 1)
        return pair // columns, pair % columns

    def permute(chunk, rows, moved, shuffle):
        chunk = jnp.minimum(chunk, chunks - 1)
        order = perm_ref[pl.ds(meta[0, chunk], 1), :]
        g_ids = lax.broadcasted_iota(jnp.int32, (g, g), 0)
        shuffle[...] = jnp.where(g_ids == order, 1.0, 0.0).astype(jnp.bfloat16)
        for p in range(CHUNK):
            row, col = row_col(table[chunk * CHUNK + p])
            rows[p * 16:(p + 1) * 16, :] = val_ref[col]
            rows[half + p * 16:half + (p + 1) * 16, :] = cond_ref[row]
        moved[...] = jnp.dot(
            rows[...], shuffle[...], preferred_element_type=jnp.float32
        ).astype(jnp.bfloat16)

    def multiply(chunk, moved):
        chunk = jnp.minimum(chunk, chunks - 1)
        carried = lax.dot_general(
            moved[:half, :], w_ref[meta[1, chunk]], (((1,), (1,)), ((), ())),
            preferred_element_type=jnp.float32,
        ).astype(jnp.bfloat16)
        products = -lax.dot_general(
            moved[half:, :], carried, (((1,), (1,)), ((), ())),
            preferred_element_type=jnp.float32,
        )
        for p in range(CHUNK):
            row, col = row_col(table[chunk * CHUNK + p])
            group = col & 7
            turned = pltpu.roll(
                products[p * 16:(p + 1) * 16, :], ((group - p + 8) & 7) * 16, 1
            ).astype(jnp.bfloat16)
            at = pl.ds(pl.multiple_of((col >> 3) * 128, 128), 128)
            out_ref[row, :, at] = jnp.where(lane_group == group, turned, out_ref[row, :, at])

    @pl.when(chunks > 0)
    def _():
        permute(0, rows_a, moved_a, shuffle_a)

        def two_chunks(i, carry):
            permute(2 * i + 1, rows_b, moved_b, shuffle_b)
            multiply(2 * i, moved_a)
            permute(2 * i + 2, rows_a, moved_a, shuffle_a)
            multiply(2 * i + 1, moved_b)
            return carry

        lax.fori_loop(0, (chunks + 1) // 2, two_chunks, 0)


def owner_products(table, meta, val_t, cond_t, w_store, g_perm):
    rows, band_pairs, g = cond_t.shape
    columns = val_t.shape[0]
    vmem = pl.BlockSpec(memory_space=pltpu.VMEM)
    smem = pl.BlockSpec(memory_space=pltpu.SMEM)
    return pl.pallas_call(
        owner_kernel,
        out_shape=jax.ShapeDtypeStruct((rows, band_pairs, columns * band_pairs), jnp.bfloat16),
        in_specs=[smem, smem, vmem, vmem, vmem, vmem],
        out_specs=vmem,
        scratch_shapes=[
            *[pltpu.VMEM((2 * CHUNK * band_pairs, g), jnp.bfloat16)] * 4,
            *[pltpu.VMEM((g, g), jnp.bfloat16)] * 2,
        ],
        compiler_params=pltpu.CompilerParams(vmem_limit_bytes=48 * 1024 * 1024),
        cost_estimate=pl.CostEstimate(
            flops=10_000_000_000, bytes_accessed=8_000_000, transcendentals=0
        ),
    )(table, meta, val_t, cond_t, w_store, g_perm)


def gather_kernel(owners, peers, q_ref, cond_ref, val_ref, q_out, cond_out, val_out,
                  q_send, q_recv, cond_send, cond_recv, val_send, val_recv, own_sem):
    a, p = lax.axis_index("ka"), lax.axis_index("kp")
    ahead, behind = lax.rem(p + 1, peers), lax.rem(p + peers - 1, peers)
    width = val_ref.shape[0]
    barrier = pltpu.get_barrier_semaphore()
    for step in range(1, owners):
        pl.semaphore_signal(
            barrier, inc=1, device_id=(lax.rem(a + step, owners), p), device_id_type=MESH
        )
    for other in (ahead, behind):
        pl.semaphore_signal(barrier, inc=1, device_id=(a, other), device_id_type=MESH)
    pl.semaphore_wait(barrier, owners + 1)
    copies = []
    for source, target, send, recv in (
        (q_ref, q_out, q_send, q_recv), (cond_ref, cond_out, cond_send, cond_recv)
    ):
        for step in range(1, owners):
            copy = pltpu.make_async_remote_copy(
                src_ref=source, dst_ref=target.at[a],
                send_sem=send.at[step - 1], recv_sem=recv.at[step - 1],
                device_id=(lax.rem(a + step, owners), p), device_id_type=MESH,
            )
            copy.start()
            copies.append(copy)
        if source is q_ref:
            copy = pltpu.make_async_remote_copy(
                src_ref=val_ref, dst_ref=val_out.at[pl.ds(width, width)],
                send_sem=val_send, recv_sem=val_recv,
                device_id=(a, ahead), device_id_type=MESH,
            )
            copy.start()
            copies.append(copy)
    own = [
        pltpu.make_async_copy(q_ref, q_out.at[a], own_sem.at[0]),
        pltpu.make_async_copy(cond_ref, cond_out.at[a], own_sem.at[1]),
        pltpu.make_async_copy(val_ref, val_out.at[pl.ds(0, width)], own_sem.at[2]),
    ]
    for copy in own:
        copy.start()
    for copy in own:
        copy.wait()
    for copy in copies:
        copy.wait()


def gathered(owners, peers, q_table, cond_t, val_t):
    anywhere = pl.BlockSpec(memory_space=pl.ANY)
    dma = pltpu.SemaphoreType.DMA
    return pl.pallas_call(
        functools.partial(gather_kernel, owners, peers),
        out_shape=(
            jax.ShapeDtypeStruct((owners, *q_table.shape), q_table.dtype),
            jax.ShapeDtypeStruct((owners, *cond_t.shape), cond_t.dtype),
            jax.ShapeDtypeStruct((2 * val_t.shape[0], *val_t.shape[1:]), val_t.dtype),
        ),
        in_specs=[anywhere] * 3,
        out_specs=(anywhere,) * 3,
        scratch_shapes=[
            dma((owners - 1,)), dma((owners - 1,)), dma((owners - 1,)), dma((owners - 1,)),
            dma, dma, dma((3,)),
        ],
        compiler_params=pltpu.CompilerParams(collective_id=0, has_side_effects=True),
    )(q_table, cond_t, val_t)


def return_kernel(owners, parts_ref, out_ref, landed, send, recv, own_sem):
    a, p = lax.axis_index("ka"), lax.axis_index("kp")
    barrier = pltpu.get_barrier_semaphore()
    for step in range(1, owners):
        pl.semaphore_signal(
            barrier, inc=1, device_id=(lax.rem(a + step, owners), p), device_id_type=MESH
        )
    pl.semaphore_wait(barrier, owners - 1)
    copies = []
    for step in range(1, owners):
        peer = lax.rem(a + step, owners)
        copy = pltpu.make_async_remote_copy(
            src_ref=parts_ref.at[peer], dst_ref=landed.at[step],
            send_sem=send.at[step - 1], recv_sem=recv.at[step - 1],
            device_id=(peer, p), device_id_type=MESH,
        )
        copy.start()
        copies.append(copy)
    own = pltpu.make_async_copy(parts_ref.at[a], landed.at[0], own_sem)
    own.start()
    own.wait()
    out_ref[...] = landed[0].astype(jnp.float32)
    for step in range(1, owners):
        copies[step - 1].wait()
        out_ref[...] += landed[step].astype(jnp.float32)


def returned(owners, parts):
    dma = pltpu.SemaphoreType.DMA
    return pl.pallas_call(
        functools.partial(return_kernel, owners),
        out_shape=jax.ShapeDtypeStruct(parts.shape[1:], jnp.float32),
        in_specs=[pl.BlockSpec(memory_space=pl.ANY)],
        out_specs=pl.BlockSpec(memory_space=pltpu.VMEM),
        scratch_shapes=[
            pltpu.VMEM(parts.shape, parts.dtype), dma((owners - 1,)), dma((owners - 1,)), dma,
        ],
        compiler_params=pltpu.CompilerParams(
            collective_id=1, has_side_effects=True, vmem_limit_bytes=32 * 1024 * 1024
        ),
    )(parts)


def per_device(cond_pairs, val_pairs, w_store, q_table, q_to_irr, g_perm, home_slot):
    owners = lax.axis_size("ka")
    peers = lax.axis_size("kp")
    per_owner = w_store.shape[0]
    row_count = cond_pairs.shape[0]
    band_pairs = cond_pairs.shape[2]
    q_all, cond_t, val_t = gathered(
        owners, peers, q_table, cond_pairs.transpose(0, 2, 1), val_pairs.transpose(0, 2, 1)
    )
    cond_t = cond_t.reshape(owners * row_count, band_pairs, -1)
    capacity = owners * 2 * (3 * row_count * row_count // 2)
    table, meta = pair_lists(q_all, q_to_irr, home_slot, per_owner, capacity)
    parts = owner_products(table, meta, val_t, cond_t, w_store, g_perm)
    columns = val_t.shape[0] * band_pairs
    parts = parts.reshape(owners, row_count * band_pairs, columns)
    return returned(owners, parts)


def solution(mesh):
    placed = (
        P(("ka", "kp"), None, None),
        P("kp", None, None),
        P("ka", None, None),
        P(("ka", "kp"), None),
        P(),
        P(),
        P(),
    )
    return jax.shard_map(
        per_device, mesh=mesh, in_specs=placed, out_specs=P(("ka", "kp"), None), check_vma=False
    )
```

time: 127 us -> 92 us (0.72)
  the two profiles are of different devices: /device:TPU:0 before, /device:TPU:9 now
where the time goes in v2:
time: 92 us; the launch traced here: 90.5 us
  Pallas kernels  79.7 us (87%)
  local copies, waits for them, and re-layouts  6.18 us (7%)
  other arithmetic  4.28 us (5%)
    pallas_call x1, Pallas kernels, returned(): pl.pallas_call(functools.partial(return_kernel, owners), out_shape=jax.Sh...  32 us
    pallas_call x1, Pallas kernels, owner_products(): pl.pallas_call(owner_kernel, out_shape=jax.ShapeDtypeStruct((rows, band_p...  25.2 us
    pallas_call x1, Pallas kernels, gathered(): pl.pallas_call(functools.partial(gather_kernel, owners, peers), out_shape...  22.5 us
    unnamed x7, local copies, waits for them, and re-layouts  4.01 us

profile of v2, /device:TPU:9, one launch (start us, length us, event | category | flops | bytes accessed | tf_op | source)
XLA Modules:
  0.0 90.5 jit_solution(16271822050419791620)
XLA Ops:
  0.0 0.8 select_reduce_fusion.2
  0.8 0.1 convert_reduce_fusion.2
  0.9 0.1 select_reduce_fusion.3
  1.1 0.1 eq.90
  1.1 0.1 eq.91
  1.2 22.5 %shard_map.73 = (s32[8,4,64]{2,1,0:T(4,128)}, bf16[8,4,16,512]{3,2,1,0:T(8,128)(2,1)}, bf16[64,16,512]{2,1,0:T(8,128)(2,1)}) custom-call(s32[4,64]{1,0:T(4,128)} %q_ref.1, bf16[4,16,512]{2,1,0:T(8,128)(2,1)} %bitcast.17, bf16[32,16,512]{2,1,0:T(8,128)(2,1)} %bitcast.16), custom_call_target="tpu_custom_call" | custom-call | tf_op jit(solution)/shard_map/pallas_call | solution.py:200
  23.7 0.8 eq.77
  24.5 1.3 %convert_reduce_fusion.1 = (s32[32]{0:T(128)S(1)}, s32[32,16]{1,0:T(8,128)S(1)}) fusion(s32[16,128]{1,0:T(8,128)S(1)} %eq.77, s32[32]{0:T(128)S(1)} %get-tuple-element.14), kind=kLoop, calls=%fused_computation.4 | loop fusion | flops 261600 | bytes 10496 | tf_op jit(solution)/shard_map/reduce_sum | solution.py:47
  25.8 0.6 fusion.7
  26.4 0.1 select_reduce_fusion.7
  26.5 0.7 pad.2.clone
  27.3 0.1 select_reduce_fusion.6
  27.4 0.1 add_add_fusion.meta
  27.4 0.1 copy.9
  27.5 0.1 select_reduce_fusion.1
  27.7 0.1 copy.10
  27.7 0.1 bitcast_compare_fusion
  27.9 0.2 convolution_convert_fusion
  28.1 0.2 fusion
  28.2 0.6 select_reduce_fusion
  28.9 0.1 reshape.154
  28.9 0.1 slice_reduce_fusion
  29.1 0.1 broadcast_in_dim.152
  29.1 0.1 broadcast_in_dim.153
  29.2 0.0 copy-start
  29.3 1.2 %copy-done = bf16[64,16,512]{2,1,0:T(8,128)(2,1)S(1)} copy-done((bf16[64,16,512]{2,1,0:T(8,128)(2,1)S(1)}, bf16[64,16,512]{2,1,0:T(8,128)(2,1)}, u32[]{:S(2)}) %copy-start) | copy-done | bytes 1048600
  30.5 0.0 copy-start.1
  30.5 1.0 %copy-done.1 = s32[256,512]{1,0:T(8,128)S(1)} copy-done((s32[256,512]{1,0:T(8,128)S(1)}, s32[256,512]{1,0:T(8,128)}, u32[]{:S(2)}) %copy-start.1) | copy-done | bytes 524312
  31.5 0.0 copy-start.2
  31.5 1.0 %copy-done.2 = bf16[8,4,16,512]{3,2,1,0:T(8,128)(2,1)S(1)} copy-done((bf16[8,4,16,512]{3,2,1,0:T(8,128)(2,1)S(1)}, bf16[8,4,16,512]{3,2,1,0:T(8,128)(2,1)}, u32[]{:S(2)}) %copy-start.2) | copy-done | bytes 524312
  32.6 25.2 %shard_map.74 = bf16[32,16,1024]{2,1,0:T(8,128)(2,1)S(1)} custom-call(s32[640]{0:T(1024)S(1)} %fusion.5.table, s32[3,80]{1,0:T(4,128)S(1)} %add_add_fusion.meta, bf16[64,16,512]{2,1,0:T(8,128)(2,1)S(1)} %copy-done, bf16[32,16,512]{2,1,0:T(8,128)(2,1)S(1)} %bitcast.14, bf16[8,512,512]{2,1,0:T(8,128)(2,1)} %w_ref.1, s32[256,512]{1,0:T(8,128)S(1)} %copy-done.1), custom_call_target="tpu_custom_call" | custom-call | flops 10000000000 | bytes 8000000 | tf_op jit(solution)/shard_map/pallas_call | solution.py:135
  57.7 32.0 %shard_map.75 = f32[64,1024]{1,0:T(8,128)S(1)} custom-call(bf16[8,64,1024]{2,1,0:T(8,128)(2,1)S(1)} %bitcast.13), custom_call_target="tpu_custom_call" | custom-call | tf_op jit(solution)/shard_map/pallas_call | solution.py:246
  89.7 0.7 copy.14
  (8 shorter events, 0.1 us)
Async XLA Ops:
  29.2 1.2 %copy-start = (bf16[64,16,512]{2,1,0:T(8,128)(2,1)S(1)}, bf16[64,16,512]{2,1,0:T(8,128)(2,1)}, u32[]{:S(2)}) copy-start(bf16[64,16,512]{2,1,0:T(8,128)(2,1)} %get-tuple-element.9.val_ref) | copy-start | bytes 3145732
  30.5 1.0 %copy-start.1 = (s32[256,512]{1,0:T(8,128)S(1)}, s32[256,512]{1,0:T(8,128)}, u32[]{:S(2)}) copy-start(s32[256,512]{1,0:T(8,128)} %perm_ref.1) | copy-start | bytes 1572868
  31.5 1.0 %copy-start.2 = (bf16[8,4,16,512]{3,2,1,0:T(8,128)(2,1)S(1)}, bf16[8,4,16,512]{3,2,1,0:T(8,128)(2,1)}, u32[]{:S(2)}) copy-start(bf16[8,4,16,512]{3,2,1,0:T(8,128)(2,1)} %get-tuple-element.10) | copy-start | bytes 1572868

commit v3 on v2

--- a/solution.py
+++ b/solution.py
@@ -67,42 +67,55 @@
     return table, jnp.stack([chunk_q, chunk_block, used])
 
 
-def owner_kernel(table, meta, val_ref, cond_ref, w_ref, perm_ref, out_ref,
-                 rows_a, rows_b, moved_a, moved_b, shuffle_a, shuffle_b):
+def owner_kernel(table, meta, val_any, cond_any, w_any, perm_any, out_ref,
+                 val_ref, cond_ref, w_ref, perm_ref, moved_0, moved_1, moved_2,
+                 carried_0, carried_1, carried_2, sems):
+    loads = [
+        pltpu.make_async_copy(source, target, sems.at[n])
+        for n, (source, target) in enumerate(
+            ((perm_any, perm_ref), (val_any, val_ref), (cond_any, cond_ref), (w_any, w_ref))
+        )
+    ]
+    for load in loads:
+        load.start()
     half = CHUNK * 16
     g = w_ref.shape[1]
     columns = val_ref.shape[0]
     chunks = meta[2, 0]
     lane_group = lax.broadcasted_iota(jnp.int32, (16, 128), 1) // 16
     out_ref[...] = jnp.zeros_like(out_ref)
+    for load in loads:
+        load.wait()
 
     def row_col(pair):
         if columns & (columns - 1) == 0:
             return pair >> (columns.bit_length() - 1), pair & (columns - 1)
         return pair // columns, pair % columns
 
-    def permute(chunk, rows, moved, shuffle):
+    def permute(chunk):
         chunk = jnp.minimum(chunk, chunks - 1)
         order = perm_ref[pl.ds(meta[0, chunk], 1), :]
         g_ids = lax.broadcasted_iota(jnp.int32, (g, g), 0)
-        shuffle[...] = jnp.where(g_ids == order, 1.0, 0.0).astype(jnp.bfloat16)
+        shuffle = jnp.where(g_ids == order, 1.0, 0.0).astype(jnp.bfloat16)
+        val_rows, cond_rows = [], []
         for p in range(CHUNK):
             row, col = row_col(table[chunk * CHUNK + p])
-            rows[p * 16:(p + 1) * 16, :] = val_ref[col]
-            rows[half + p * 16:half + (p + 1) * 16, :] = cond_ref[row]
-        moved[...] = jnp.dot(
-            rows[...], shuffle[...], preferred_element_type=jnp.float32
-        ).astype(jnp.bfloat16)
-
-    def multiply(chunk, moved):
+            val_rows.append(val_ref[col])
+            cond_rows.append(cond_ref[row])
+        rows = jnp.concatenate(val_rows + cond_rows, axis=0)
+        return jnp.dot(rows, shuffle, preferred_element_type=jnp.float32).astype(jnp.bfloat16)
+
+    def carry_over(chunk, val_rows):
         chunk = jnp.minimum(chunk, chunks - 1)
-        carried = lax.dot_general(
-            moved[:half, :], w_ref[meta[1, chunk]], (((1,), (1,)), ((), ())),
+        return lax.dot_general(
+            val_rows, w_ref[meta[1, chunk]], (((1,), (1,)), ((), ())),
             preferred_element_type=jnp.float32,
         ).astype(jnp.bfloat16)
+
+    def multiply(chunk, cond_rows, carried):
+        chunk = jnp.minimum(chunk, chunks - 1)
         products = -lax.dot_general(
-            moved[half:, :], carried, (((1,), (1,)), ((), ())),
-            preferred_element_type=jnp.float32,
+            cond_rows, carried, (((1,), (1,)), ((), ())), preferred_element_type=jnp.float32
         )
         for p in range(CHUNK):
             row, col = row_col(table[chunk * CHUNK + p])
@@ -113,33 +126,42 @@
             at = pl.ds(pl.multiple_of((col >> 3) * 128, 128), 128)
             out_ref[row, :, at] = jnp.where(lane_group == group, turned, out_ref[row, :, at])
 
+    moved = (moved_0, moved_1, moved_2)
+    carried = (carried_0, carried_1, carried_2)
+
     @pl.when(chunks > 0)
     def _():
-        permute(0, rows_a, moved_a, shuffle_a)
-
-        def two_chunks(i, carry):
-            permute(2 * i + 1, rows_b, moved_b, shuffle_b)
-            multiply(2 * i, moved_a)
-            permute(2 * i + 2, rows_a, moved_a, shuffle_a)
-            multiply(2 * i + 1, moved_b)
-            return carry
-
-        lax.fori_loop(0, (chunks + 1) // 2, two_chunks, 0)
+        moved_0[...] = permute(0)
+        moved_1[...] = permute(1)
+        carried_0[...] = carry_over(0, moved_0[:half, :])
+
+        def three_chunks(i, state):
+            for u in range(3):
+                chunk, v, w = 3 * i + u, (u + 1) % 3, (u + 2) % 3
+                multiply(chunk, moved[u][half:, :], carried[u][...])
+                carried[v][...] = carry_over(chunk + 1, moved[v][:half, :])
+                moved[w][...] = permute(chunk + 2)
+            return state
+
+        lax.fori_loop(0, (chunks + 2) // 3, three_chunks, 0)
 
 
 def owner_products(table, meta, val_t, cond_t, w_store, g_perm):
     rows, band_pairs, g = cond_t.shape
     columns = val_t.shape[0]
     vmem = pl.BlockSpec(memory_space=pltpu.VMEM)
+    anywhere = pl.BlockSpec(memory_space=pl.ANY)
     smem = pl.BlockSpec(memory_space=pltpu.SMEM)
     return pl.pallas_call(
         owner_kernel,
         out_shape=jax.ShapeDtypeStruct((rows, band_pairs, columns * band_pairs), jnp.bfloat16),
-        in_specs=[smem, smem, vmem, vmem, vmem, vmem],
+        in_specs=[smem, smem, anywhere, anywhere, anywhere, anywhere],
         out_specs=vmem,
         scratch_shapes=[
-            *[pltpu.VMEM((2 * CHUNK * band_pairs, g), jnp.bfloat16)] * 4,
-            *[pltpu.VMEM((g, g), jnp.bfloat16)] * 2,
+            *[pltpu.VMEM(x.shape, x.dtype) for x in (val_t, cond_t, w_store, g_perm)],
+            *[pltpu.VMEM((2 * CHUNK * band_pairs, g), jnp.bfloat16)] * 3,
+            *[pltpu.VMEM((CHUNK * band_pairs, g), jnp.bfloat16)] * 3,
+            pltpu.SemaphoreType.DMA((4,)),
         ],
         compiler_params=pltpu.CompilerParams(vmem_limit_bytes=48 * 1024 * 1024),
         cost_estimate=pl.CostEstimate(
@@ -149,54 +171,85 @@
 
 
 def gather_kernel(owners, peers, q_ref, cond_ref, val_ref, q_out, cond_out, val_out,
-                  q_send, q_recv, cond_send, cond_recv, val_send, val_recv, own_sem):
+                  send, recv, near_send, near_recv, pass_send, pass_recv, own_sem):
     a, p = lax.axis_index("ka"), lax.axis_index("kp")
+    chips = owners // 2
+    chip, core = a // 2, lax.rem(a, 2)
+    near = a + 1 - 2 * core
     ahead, behind = lax.rem(p + 1, peers), lax.rem(p + peers - 1, peers)
-    width = val_ref.shape[0]
+    half = val_ref.shape[0] // 2
     barrier = pltpu.get_barrier_semaphore()
-    for step in range(1, owners):
+    for step in range(1, chips):
         pl.semaphore_signal(
-            barrier, inc=1, device_id=(lax.rem(a + step, owners), p), device_id_type=MESH
-        )
-    for other in (ahead, behind):
-        pl.semaphore_signal(barrier, inc=1, device_id=(a, other), device_id_type=MESH)
-    pl.semaphore_wait(barrier, owners + 1)
-    copies = []
-    for source, target, send, recv in (
-        (q_ref, q_out, q_send, q_recv), (cond_ref, cond_out, cond_send, cond_recv)
-    ):
-        for step in range(1, owners):
-            copy = pltpu.make_async_remote_copy(
-                src_ref=source, dst_ref=target.at[a],
-                send_sem=send.at[step - 1], recv_sem=recv.at[step - 1],
-                device_id=(lax.rem(a + step, owners), p), device_id_type=MESH,
+            barrier, inc=1, device_id=(lax.rem(chip + step, chips) * 2 + core, p),
+            device_id_type=MESH,
+        )
+    for place in ((near, p), (a, ahead), (a, behind)):
+        pl.semaphore_signal(barrier, inc=1, device_id=place, device_id_type=MESH)
+    pl.semaphore_wait(barrier, chips + 2)
+
+    def started(source, target, sems, place):
+        copy = pltpu.make_async_remote_copy(
+            src_ref=source, dst_ref=target, send_sem=sems[0], recv_sem=sems[1],
+            device_id=place, device_id_type=MESH,
+        )
+        copy.start()
+        return copy
+
+    arrays = ((q_ref, q_out), (cond_ref, cond_out))
+    far, done = [], []
+    for kind, (source, target) in enumerate(arrays):
+        if kind == 1:
+            part = pl.ds(core * half, half)
+            landing = pl.ds(2 * half + core * half, half)
+            last = 2 * (chips - 1)
+            panel = started(
+                val_ref.at[part], val_out.at[landing], (send.at[last], recv.at[last]), (a, ahead)
             )
-            copy.start()
-            copies.append(copy)
-        if source is q_ref:
-            copy = pltpu.make_async_remote_copy(
-                src_ref=val_ref, dst_ref=val_out.at[pl.ds(width, width)],
-                send_sem=val_send, recv_sem=val_recv,
-                device_id=(a, ahead), device_id_type=MESH,
-            )
-            copy.start()
-            copies.append(copy)
+        for step in range(1, chips):
+            at = kind * (chips - 1) + step - 1
+            place = (lax.rem(chip + step, chips) * 2 + core, p)
+            far.append(started(source, target.at[a], (send.at[at], recv.at[at]), place))
+        done.append(
+            started(source, target.at[a], (near_send.at[kind], near_recv.at[kind]), (near, p))
+        )
     own = [
         pltpu.make_async_copy(q_ref, q_out.at[a], own_sem.at[0]),
         pltpu.make_async_copy(cond_ref, cond_out.at[a], own_sem.at[1]),
-        pltpu.make_async_copy(val_ref, val_out.at[pl.ds(0, width)], own_sem.at[2]),
+        pltpu.make_async_copy(val_ref, val_out.at[pl.ds(0, 2 * half)], own_sem.at[2]),
     ]
     for copy in own:
         copy.start()
+    for kind, (source, target) in enumerate(arrays):
+        for step in range(1, chips):
+            at = kind * (chips - 1) + step - 1
+            far[at].wait_recv()
+            origin = lax.rem(chip + chips - step, chips) * 2 + core
+            done.append(
+                started(
+                    target.at[origin], target.at[origin],
+                    (pass_send.at[at], pass_recv.at[at]), (near, p),
+                )
+            )
+    panel.wait_recv()
+    done.append(
+        started(
+            val_out.at[landing], val_out.at[landing],
+            (pass_send.at[last], pass_recv.at[last]), (near, p),
+        )
+    )
     for copy in own:
         copy.wait()
-    for copy in copies:
+    for copy in far + [panel]:
+        copy.wait_send()
+    for copy in done:
         copy.wait()
 
 
 def gathered(owners, peers, q_table, cond_t, val_t):
     anywhere = pl.BlockSpec(memory_space=pl.ANY)
     dma = pltpu.SemaphoreType.DMA
+    count = owners - 1
     return pl.pallas_call(
         functools.partial(gather_kernel, owners, peers),
         out_shape=(
@@ -207,8 +260,8 @@
         in_specs=[anywhere] * 3,
         out_specs=(anywhere,) * 3,
         scratch_shapes=[
-            dma((owners - 1,)), dma((owners - 1,)), dma((owners - 1,)), dma((owners - 1,)),
-            dma, dma, dma((3,)),
+            dma((count,)), dma((count,)), dma((2,)), dma((2,)), dma((count,)), dma((count,)),
+            dma((3,)),
         ],
         compiler_params=pltpu.CompilerParams(collective_id=0, has_side_effects=True),
     )(q_table, cond_t, val_t)

time: 92 us -> 83.3 us (0.905); the launches traced: 90.5 us -> 83.3 us
  Pallas kernels: 79.7 us -> 72.5 us
    pallas_call x1, Pallas kernels: 25.2 us -> 21.3 us  [owner_products(): pl.pallas_call(owner_kernel, out_shape=jax.ShapeDtypeStruct((rows, band_p...]
    pallas_call x1, Pallas kernels: 32 us -> 29.4 us  [returned(): pl.pallas_call(functools.partial(return_kernel, owners), out_shape=jax.Sh...]
where the time goes in v3:
time: 83.3 us
  Pallas kernels  72.5 us (87%)
  local copies, waits for them, and re-layouts  6.18 us (7%)
  other arithmetic  4.28 us (5%)
    pallas_call x1, Pallas kernels, returned(): pl.pallas_call(functools.partial(return_kernel, owners), out_shape=jax.Sh...  29.4 us
    pallas_call x1, Pallas kernels, gathered(): pl.pallas_call(functools.partial(gather_kernel, owners, peers), out_shape...  21.8 us
    pallas_call x1, Pallas kernels, owner_products(): pl.pallas_call(owner_kernel, out_shape=jax.ShapeDtypeStruct((rows, band_p...  21.3 us
    unnamed x7, local copies, waits for them, and re-layouts  4.01 us

profile of v3, /device:TPU:9, one launch (start us, length us, event | category | flops | bytes accessed | tf_op | source)
XLA Modules:
  0.0 83.3 jit_solution(9276993817164475524)
XLA Ops:
  0.0 0.8 select_reduce_fusion.2
  0.8 0.1 convert_reduce_fusion.2
  0.9 0.1 select_reduce_fusion.3
  1.1 0.1 eq.90
  1.1 0.1 eq.91
  1.2 21.8 %shard_map.73 = (s32[8,4,64]{2,1,0:T(4,128)}, bf16[8,4,16,512]{3,2,1,0:T(8,128)(2,1)}, bf16[64,16,512]{2,1,0:T(8,128)(2,1)}) custom-call(s32[4,64]{1,0:T(4,128)} %q_ref.1, bf16[4,16,512]{2,1,0:T(8,128)(2,1)} %bitcast.17, bf16[32,16,512]{2,1,0:T(8,128)(2,1)} %bitcast.16), custom_call_target="tpu_custom_call" | custom-call | tf_op jit(solution)/shard_map/pallas_call | solution.py:253
  23.0 0.8 eq.77
  23.8 1.3 %convert_reduce_fusion.1 = (s32[32]{0:T(128)S(1)}, s32[32,16]{1,0:T(8,128)S(1)}) fusion(s32[16,128]{1,0:T(8,128)S(1)} %eq.77, s32[32]{0:T(128)S(1)} %get-tuple-element.14), kind=kLoop, calls=%fused_computation.4 | loop fusion | flops 261600 | bytes 10496 | tf_op jit(solution)/shard_map/reduce_sum | solution.py:47
  25.1 0.6 fusion.7
  25.7 0.1 select_reduce_fusion.7
  25.8 0.7 pad.2.clone
  26.6 0.1 select_reduce_fusion.6
  26.7 0.1 add_add_fusion.meta
  26.7 0.1 copy.9
  26.8 0.1 select_reduce_fusion.1
  27.0 0.1 copy.10
  27.0 0.1 bitcast_compare_fusion
  27.2 0.2 convolution_convert_fusion
  27.4 0.2 fusion
  27.5 0.6 select_reduce_fusion
  28.2 0.1 reshape.154
  28.2 0.1 slice_reduce_fusion
  28.4 0.1 broadcast_in_dim.152
  28.4 0.1 broadcast_in_dim.153
  28.5 0.0 copy-start
  28.6 1.2 %copy-done = bf16[64,16,512]{2,1,0:T(8,128)(2,1)S(1)} copy-done((bf16[64,16,512]{2,1,0:T(8,128)(2,1)S(1)}, bf16[64,16,512]{2,1,0:T(8,128)(2,1)}, u32[]{:S(2)}) %copy-start) | copy-done | bytes 1048600
  29.8 0.0 copy-start.1
  29.8 1.0 %copy-done.1 = s32[256,512]{1,0:T(8,128)S(1)} copy-done((s32[256,512]{1,0:T(8,128)S(1)}, s32[256,512]{1,0:T(8,128)}, u32[]{:S(2)}) %copy-start.1) | copy-done | bytes 524312
  30.8 0.0 copy-start.2
  30.8 1.0 %copy-done.2 = bf16[8,4,16,512]{3,2,1,0:T(8,128)(2,1)S(1)} copy-done((bf16[8,4,16,512]{3,2,1,0:T(8,128)(2,1)S(1)}, bf16[8,4,16,512]{3,2,1,0:T(8,128)(2,1)}, u32[]{:S(2)}) %copy-start.2) | copy-done | bytes 524312
  31.9 21.3 %shard_map.74 = bf16[32,16,1024]{2,1,0:T(8,128)(2,1)S(1)} custom-call(s32[640]{0:T(1024)S(1)} %fusion.5.table, s32[3,80]{1,0:T(4,128)S(1)} %add_add_fusion.meta, bf16[64,16,512]{2,1,0:T(8,128)(2,1)S(1)} %copy-done, bf16[32,16,512]{2,1,0:T(8,128)(2,1)S(1)} %bitcast.14, bf16[8,512,512]{2,1,0:T(8,128)(2,1)} %w_any.1, s32[256,512]{1,0:T(8,128)S(1)} %copy-done.1), custom_call_target="tpu_custom_call" | custom-call | flops 10000000000 | bytes 8000000 | tf_op jit(solution)/shard_map/pallas_call | solution.py:155
  53.2 29.4 %shard_map.75 = f32[64,1024]{1,0:T(8,128)S(1)} custom-call(bf16[8,64,1024]{2,1,0:T(8,128)(2,1)S(1)} %bitcast.13), custom_call_target="tpu_custom_call" | custom-call | tf_op jit(solution)/shard_map/pallas_call | solution.py:299
  82.6 0.7 copy.14
  (8 shorter events, 0.1 us)
Async XLA Ops:
  28.5 1.2 %copy-start = (bf16[64,16,512]{2,1,0:T(8,128)(2,1)S(1)}, bf16[64,16,512]{2,1,0:T(8,128)(2,1)}, u32[]{:S(2)}) copy-start(bf16[64,16,512]{2,1,0:T(8,128)(2,1)} %get-tuple-element.9.val_any) | copy-start | bytes 3145732
  29.8 1.0 %copy-start.1 = (s32[256,512]{1,0:T(8,128)S(1)}, s32[256,512]{1,0:T(8,128)}, u32[]{:S(2)}) copy-start(s32[256,512]{1,0:T(8,128)} %perm_any.1) | copy-start | bytes 1572868
  30.8 1.0 %copy-start.2 = (bf16[8,4,16,512]{3,2,1,0:T(8,128)(2,1)S(1)}, bf16[8,4,16,512]{3,2,1,0:T(8,128)(2,1)}, u32[]{:S(2)}) copy-start(bf16[8,4,16,512]{3,2,1,0:T(8,128)(2,1)} %get-tuple-element.10) | copy-start | bytes 1572868
